TPU v7x, 256 devices: a whole 4x4x8 slice. The times are simulated.
256 devices in a mesh: seq: 32 (over z, y), head: 8 (over x, core).
Axes of the slice: x: 4, y: 4, z: 8, core: 2. Of those that a mesh axis runs over, the one named last changes fastest.
Arguments:
- query: bfloat16 [49152, 3072], P(('seq', 'head')), may hold values from -40 to 40
- key: bfloat16 [49152, 3072], P(('seq', 'head')), may hold values from -4 to 4
- value: bfloat16 [49152, 3072], P(('seq', 'head')), may hold values from -6 to 6
- raster_to_tile: int32 [49152], P(('seq', 'head')), may hold values from 0 to 49151, as said below
- window_list: int32 [128, 4], P('seq'), may hold values from 0 to 127, as said below
- valid_count: int32 [128], replicated, may hold values from 96 to 384
Outputs:
- attended: bfloat16 [49152, 3072], P(('seq', 'head'))
Inputs may be any that keep to these rules, and one draw needn't show every extreme that they name: `raster_to_tile`: A permutation of the slots. Raster shard d (rows d * 1536 // 8 onward, d counting seq+head) holds exactly 6 slots of every owner o, where owner o holds slots o * 1536 to (o+1) * 1536 - 1. `window_list`: row t holds t first, then 4 - 1 distinct other tiles, each within 3 tiles of t.
All inputs are finite; a program needn't handle non-finite values.
Results may differ from a plain program's by a relative error of at most 0.0036.
Values may be sent and summed in bfloat16 or wider, within the bound.
A program may use at most 64 MiB of HBM per device.

v0:
```python
import jax
import jax.numpy as jnp
from jax import lax
from jax.sharding import PartitionSpec as P

HEAD_DIM = 128


def body(query, key, value, raster_to_tile, window_list, valid_count):
    seq_count = lax.axis_size("seq")
    head_count = lax.axis_size("head")
    seq_pos = lax.axis_index("seq")
    rows_here, width = query.shape
    part_width = width // head_count
    tile_dev, win = window_list.shape
    tok_dev = rows_here * head_count
    tile = tok_dev // tile_dev
    share = rows_here // seq_count
    reach = win - 1
    rim = reach * tile
    ext_rows = tok_dev + 2 * rim
    ext_tiles = tile_dev + 2 * reach
    heads_here = part_width // HEAD_DIM
    all_tiles = valid_count.shape[0]
    order = jnp.argsort(raster_to_tile)
    slots_sorted = raster_to_tile[order].reshape(seq_count, share)
    query_sorted = query[order].reshape(seq_count, share, head_count, part_width)
    joined = jnp.concatenate(
        [
            key.reshape(rows_here, head_count, part_width),
            value.reshape(rows_here, head_count, part_width),
        ],
        axis=2,
    )
    pair_sorted = joined[order].reshape(seq_count, share, head_count, 2 * part_width)
    zero_pair = jnp.zeros_like(pair_sorted[:1])
    wide_pair = jnp.concatenate(
        [
            jnp.concatenate([zero_pair, pair_sorted[:-1]], axis=0),
            pair_sorted,
            jnp.concatenate([pair_sorted[1:], zero_pair], axis=0),
        ],
        axis=1,
    )
    empty_slots = jnp.full((1, share), -1, jnp.int32)
    wide_slots = jnp.concatenate(
        [
            jnp.concatenate([empty_slots, slots_sorted[:-1]], axis=0),
            slots_sorted,
            jnp.concatenate([slots_sorted[1:], empty_slots], axis=0),
        ],
        axis=1,
    )
    slot_send = jnp.broadcast_to(wide_slots[:, :, None], (seq_count, 3 * share, head_count))
    query_in, pair_in, slot_in = (
        lax.all_to_all(
            lax.all_to_all(query_sorted, "seq", split_axis=0, concat_axis=0, tiled=True),
            "head",
            split_axis=2,
            concat_axis=1,
            tiled=True,
        ),
        lax.all_to_all(
            lax.all_to_all(wide_pair, "seq", split_axis=0, concat_axis=0, tiled=True),
            "head",
            split_axis=2,
            concat_axis=1,
            tiled=True,
        ),
        lax.all_to_all(
            lax.all_to_all(slot_send, "seq", split_axis=0, concat_axis=0, tiled=True),
            "head",
            split_axis=2,
            concat_axis=1,
            tiled=True,
        ),
    )
    middle = slot_in.reshape(seq_count, head_count, 3, share)[:, :, 1, :]
    local = middle.reshape(tok_dev) - seq_pos * tok_dev
    place = jnp.zeros((tok_dev,), jnp.int32).at[local].set(jnp.arange(tok_dev, dtype=jnp.int32))
    query_tile = query_in.reshape(tok_dev, part_width)[place]
    every_slot = slot_in.reshape(3 * tok_dev)
    shifted = every_slot - (seq_pos * tok_dev - rim)
    target = jnp.where((every_slot >= 0) & (shifted >= 0) & (shifted < ext_rows), shifted, ext_rows)
    place_ext = (
        jnp.full((ext_rows,), 3 * tok_dev, jnp.int32)
        .at[target]
        .set(jnp.arange(3 * tok_dev, dtype=jnp.int32), mode="drop")
    )
    padded = jnp.concatenate(
        [
            pair_in.reshape(3 * tok_dev, 2 * part_width),
            jnp.zeros((1, 2 * part_width), pair_in.dtype),
        ],
        axis=0,
    )
    pair_ext = padded[place_ext]
    first_tile = seq_pos * tile_dev - reach
    global_tiles = jnp.clip(first_tile + jnp.arange(ext_tiles, dtype=jnp.int32), 0, all_tiles - 1)
    key_usable = jnp.arange(tile, dtype=jnp.int32)[None, :] < valid_count[global_tiles][:, None]
    own_usable = key_usable[reach : reach + tile_dev]
    local_windows = window_list - first_tile
    query_blocks = query_tile.reshape(tile_dev, tile, heads_here, HEAD_DIM)
    pair_blocks = pair_ext.reshape(ext_tiles, tile, 2, heads_here, HEAD_DIM)
    scale = HEAD_DIM ** (-0.5)

    def one_tile(item):
        query_blk, windows, query_usable = item
        picked = pair_blocks[windows]
        keys_blk = picked[:, :, 0].reshape(win * tile, heads_here, HEAD_DIM)
        values_blk = picked[:, :, 1].reshape(win * tile, heads_here, HEAD_DIM)
        usable = key_usable[windows].reshape(win * tile)
        scores = (
            jnp.einsum("qhd,khd->hqk", query_blk, keys_blk, preferred_element_type=jnp.float32)
            * scale
        )
        scores = jnp.where(usable[None, None, :], scores, -jnp.inf)
        top = jnp.max(scores, axis=2, keepdims=True)
        weights = jnp.exp(scores - top)
        total = jnp.sum(weights, axis=2)
        mixed = jnp.einsum(
            "hqk,khd->qhd",
            weights.astype(jnp.bfloat16),
            values_blk,
            preferred_element_type=jnp.float32,
        )
        mixed = mixed / jnp.transpose(total)[:, :, None]
        mixed = jnp.where(query_usable[:, None, None], mixed, 0.0)
        return mixed.astype(jnp.bfloat16).reshape(tile, part_width)

    out_tile = lax.map(one_tile, (query_blocks, local_windows, own_usable)).reshape(
        tok_dev, part_width
    )
    outgoing = out_tile[local].reshape(seq_count, head_count, share, 1, part_width)
    arrived = lax.all_to_all(
        lax.all_to_all(outgoing, "seq", split_axis=0, concat_axis=0, tiled=True),
        "head",
        split_axis=1,
        concat_axis=3,
        tiled=True,
    )
    sorted_rows = arrived.reshape(rows_here, width)
    inverse = (
        jnp.zeros((rows_here,), jnp.int32).at[order].set(jnp.arange(rows_here, dtype=jnp.int32))
    )
    return sorted_rows[inverse]


def solution(mesh):
    placed = (
        P(("seq", "head"), None),
        P(("seq", "head"), None),
        P(("seq", "head"), None),
        P(("seq", "head")),
        P("seq", None),
        P(),
    )
    return jax.shard_map(
        body, mesh=mesh, in_specs=placed, out_specs=P(("seq", "head"), None), check_vma=False
    )
```

profile of v0, /device:TPU:1, one launch (start us, length us, event | category | flops | bytes accessed | tf_op | source)
XLA Modules:
  0.0 554.6 jit_solution(8304889225877488797)
XLA Ops:
  0.0 3.9 sort.17
  4.0 2.0 gather_fusion.4
  6.6 20.5 %all_to_all.80 = s32[32,1,144]{2,1,0:T(1,128)S(1)} all-to-all(s32[32,1,144]{2,1,0:T(1,128)S(1)} %reshape.329), channel_id=1, replica_groups=mesh['seq'=32,'head'=8] {'seq'}, dimensions={0} | all-to-all | bytes 36864 | tf_op jit(solution)/shard_map/all_to_all | solution.py:71
  27.7 0.8 reduce.6
  28.7 0.7 reshape.331
  29.4 6.4 %all-to-all-start.3 = ((s32[8,1,576]{2,1,0:T(1,128)}), s32[8,1,576]{2,1,0:T(1,128)}, u32[]{:S(2)}, u32[]{:S(2)}) async-start(s32[8,1,576]{2,1,0:T(1,128)} %reshape.331), calls=%async_computation.3 | async-start | bytes 40960 | tf_op jit(solution)/shard_map/all_to_all | solution.py:70
  35.8 1.3 gather_fusion.6
  37.1 1.2 copy.69
  38.4 2.2 all-to-all-done.3
  40.6 4.1 all-to-all-start.4
  45.1 1.6 pad_maximum_fusion
  46.7 2.5 gather_fusion.3
  49.6 3.3 fusion.37
  52.9 21.1 %all-to-all-done.4 = bf16[32,6,8,384]{3,2,1,0:T(8,128)(2,1)S(1)} async-done(((bf16[32,6,8,384]{3,2,1,0:T(8,128)(2,1)}), bf16[32,6,8,384]{3,2,1,0:T(8,128)(2,1)S(1)}, u32[]{:S(2)}, u32[]{:S(2)}) %all-to-all-start.4) | async-done | bytes 1179680 | tf_op jit(solution)/shard_map/all_to_all | solution.py:57
  74.0 6.5 %all-to-all-start = ((bf16[32,18,8,768]{3,2,1,0:T(8,128)(2,1)}), bf16[32,18,8,768]{3,2,1,0:T(8,128)(2,1)}, u32[]{:S(2)}, u32[]{:S(2)}) async-start(bf16[32,18,8,768]{3,2,1,0:T(8,128)(2,1)} %fusion.37), calls=%async_computation | async-start | bytes 14155776 | tf_op jit(solution)/shard_map/all_to_all | solution.py:64
  80.5 1.3 copy.50
  81.8 152.8 %all-to-all-done = bf16[32,18,8,768]{3,2,1,0:T(8,128)(2,1)} async-done(((bf16[32,18,8,768]{3,2,1,0:T(8,128)(2,1)}), bf16[32,18,8,768]{3,2,1,0:T(8,128)(2,1)}, u32[]{:S(2)}, u32[]{:S(2)}) %all-to-all-start) | async-done | bytes 7077920 | tf_op jit(solution)/shard_map/all_to_all | solution.py:64
  234.5 9.1 %all-to-all-start.5 = ((bf16[32,6,8,384]{3,0,1,2:T(8,128)(2,1)}), bf16[32,6,8,384]{3,0,1,2:T(8,128)(2,1)S(1)}, u32[]{:S(2)}, u32[]{:S(2)}) async-start(bf16[32,6,8,384]{3,0,1,2:T(8,128)(2,1)} %copy.50), calls=%async_computation.5 | async-start | bytes 2359296 | tf_op jit(solution)/shard_map/all_to_all | solution.py:56
  243.7 8.3 %copy.44 = bf16[32,18,8,768]{3,0,1,2:T(8,128)(2,1)} copy(bf16[32,18,8,768]{3,2,1,0:T(8,128)(2,1)} %all-to-all-done) | data formatting | bytes 14155776 | tf_op jit(solution)/shard_map/all_to_all | solution.py:64
  252.0 8.2 %all-to-all-done.5 = bf16[32,6,8,384]{3,0,1,2:T(8,128)(2,1)S(1)} async-done(((bf16[32,6,8,384]{3,0,1,2:T(8,128)(2,1)}), bf16[32,6,8,384]{3,0,1,2:T(8,128)(2,1)S(1)}, u32[]{:S(2)}, u32[]{:S(2)}) %all-to-all-start.5) | async-done | bytes 1179680 | tf_op jit(solution)/shard_map/all_to_all | solution.py:56
  260.2 5.6 %all-to-all-start.1 = ((bf16[32,18,8,768]{3,0,1,2:T(8,128)(2,1)}), bf16[32,18,8,768]{3,0,1,2:T(8,128)(2,1)}, u32[]{:S(2)}, u32[]{:S(2)}) async-start(bf16[32,18,8,768]{3,0,1,2:T(8,128)(2,1)} %copy.44), calls=%async_computation.1 | async-start | bytes 14155776 | tf_op jit(solution)/shard_map/all_to_all | solution.py:63
  266.6 1.5 reduce.7
  269.2 6.2 %scatter_custom_fusion.1 = s32[1536]{0:T(1024)S(1)} fusion(s32[1536]{0:T(1024)S(1)} %fusion.42, s32[1536]{0:T(1024)S(1)} %iota.24, s32[]{:T(128)} %constant.29.clone.1), kind=kCustom, calls=%fused_computation.70 | custom fusion | bytes 6148 | tf_op jit(solution)/shard_map/scatter | solution.py:80
  275.5 17.6 %scatter_custom_fusion = s32[3840]{0:T(1024)S(1)} fusion(s32[4608]{0:T(1024)S(1)} %fusion.39, s32[4608]{0:T(1024)S(1)} %iota.23, s32[]{:T(128)} %constant.14.clone.1), kind=kCustom, calls=%fused_computation.63 | custom fusion | bytes 15364 | tf_op jit(solution)/shard_map/scatter | solution.py:88
  293.2 1.6 copy.51
  294.8 2.3 reshape.197
  297.1 5.3 gather_fusion.7
  302.4 3.3 reshape.319
  305.7 1.3 copy.54
  307.0 38.6 %all-to-all-done.1 = bf16[32,18,8,768]{3,0,1,2:T(8,128)(2,1)} async-done(((bf16[32,18,8,768]{3,0,1,2:T(8,128)(2,1)}), bf16[32,18,8,768]{3,0,1,2:T(8,128)(2,1)}, u32[]{:S(2)}, u32[]{:S(2)}) %all-to-all-start.1) | async-done | bytes 7077920 | tf_op jit(solution)/shard_map/all_to_all | solution.py:63
  345.6 10.9 %copy.45 = bf16[32,8,18,1,768]{4,2,1,0,3:T(8,128)(2,1)} copy(bf16[32,8,18,1,768]{4,0,2,1,3:T(8,128)(2,1)} %bitcast.5) | data formatting | bytes 14155776 | tf_op jit(solution)/shard_map/all_to_all | solution.py:63
  356.5 11.5 %reshape.193 = bf16[4608,768]{1,0:T(8,128)(2,1)} reshape(bf16[32,8,18,1,768]{4,2,1,0,3:T(8,128)(2,1)} %copy.45) | data formatting | bytes 14155776 | tf_op jit(solution)/shard_map/reshape | solution.py:92
  368.0 6.4 %concatenate.28 = bf16[4609,768]{1,0:T(8,128)(2,1)} pad(bf16[4608,768]{1,0:T(8,128)(2,1)} %reshape.193, bf16[]{:T(256)} %constant.30.clone.1), padding=0_1x0_0 | pad | bytes 14157314 | tf_op jit(solution)/shard_map/concatenate | solution.py:90
  374.3 18.8 %gather_fusion.5 = bf16[3840,768]{1,0:T(8,128)(2,1)} fusion(bf16[4609,768]{1,0:T(8,128)(2,1)} %concatenate.28, s32[4096]{0:T(1024)S(1)} %pad_clamp_fusion.1), kind=kCustom, calls=%fused_computation.5 | custom fusion | bytes 11811840 | tf_op jit(solution)/shard_map/gather | solution.py:97
  393.1 13.8 %reshape.195 = bf16[10,384,2,3,128]{4,3,2,1,0:T(4,128)(2,1)} reshape(bf16[3840,768]{1,0:T(8,128)(2,1)} %gather_fusion.5) | data formatting | bytes 11796480 | tf_op jit(solution)/shard_map/reshape | solution.py:104
  406.9 71.9 %while.11 = (s32[]{:T(128)}, bf16[4,384,384]{2,1,0:T(8,128)(2,1)S(1)}, pred[4,384]{1,0:T(4,128)(4,1)S(1)}, s32[4,4]{1,0:T(4,128)S(1)}, bf16[10,384,2,3,128]{4,3,...) while((s32[]{:T(128)}, ...), condition=%wide.region_6.7_spmd.clone, body=%wide.region_3.6_spmd.clone.sunk | while | flops 925878784 | bytes 37202520 | solution.py:131
  407.6 8.1 %gather_fusion.1 = bf16[4,384,2,3,128]{4,3,2,1,0:T(4,128)(2,1)} fusion(bf16[10,384,2,3,128]{4,3,2,1,0:T(4,128)(2,1)} %get-tuple-element.185, s32[1024]{0:T(1024)S(1)} %pad_clamp_fusion.8), kind=kCustom, calls=%fused_computation.clone.clone.1 | custom fusion | bytes 4718608 | tf_op jit(solution)/shard_map/while/body/eval_jaxpr/gather | solution.py:109
  415.6 3.0 fusion.64
  418.8 2.2 fusion.65
  421.0 1.5 fusion.66
  422.5 2.0 fusion.67
  425.6 8.1 %gather_fusion.1 = bf16[4,384,2,3,128]{4,3,2,1,0:T(4,128)(2,1)} fusion(bf16[10,384,2,3,128]{4,3,2,1,0:T(4,128)(2,1)} %get-tuple-element.185, s32[1024]{0:T(1024)S(1)} %pad_clamp_fusion.8), kind=kCustom, calls=%fused_computation.clone.clone.1 | custom fusion | bytes 4718608 | tf_op jit(solution)/shard_map/while/body/eval_jaxpr/gather | solution.py:109
  433.6 3.0 fusion.64
  436.8 2.2 fusion.65
  439.0 1.5 fusion.66
  440.5 2.0 fusion.67
  443.6 8.1 %gather_fusion.1 = bf16[4,384,2,3,128]{4,3,2,1,0:T(4,128)(2,1)} fusion(bf16[10,384,2,3,128]{4,3,2,1,0:T(4,128)(2,1)} %get-tuple-element.185, s32[1024]{0:T(1024)S(1)} %pad_clamp_fusion.8), kind=kCustom, calls=%fused_computation.clone.clone.1 | custom fusion | bytes 4718608 | tf_op jit(solution)/shard_map/while/body/eval_jaxpr/gather | solution.py:109
  451.6 3.0 fusion.64
  454.8 2.2 fusion.65
  457.0 1.5 fusion.66
  458.5 2.0 fusion.67
  461.5 8.1 %gather_fusion.1 = bf16[4,384,2,3,128]{4,3,2,1,0:T(4,128)(2,1)} fusion(bf16[10,384,2,3,128]{4,3,2,1,0:T(4,128)(2,1)} %get-tuple-element.185, s32[1024]{0:T(1024)S(1)} %pad_clamp_fusion.8), kind=kCustom, calls=%fused_computation.clone.clone.1 | custom fusion | bytes 4718608 | tf_op jit(solution)/shard_map/while/body/eval_jaxpr/gather | solution.py:109
  469.6 3.0 fusion.64
  472.8 2.2 fusion.65
  475.0 1.5 fusion.66
  476.5 2.0 fusion.67
  478.8 5.3 gather_fusion.8
  484.1 2.2 reshape.201
  486.6 40.7 %all_to_all.81 = bf16[32,8,6,1,384]{4,1,3,2,0:T(8,128)(2,1)S(1)} all-to-all(bf16[32,8,6,1,384]{4,1,3,2,0:T(8,128)(2,1)S(1)} %copy.56), channel_id=1, replica_groups=mesh['seq'=32,'head'=8] {'seq'}, dimensions={0} | all-to-all | bytes 2359296 | tf_op jit(solution)/shard_map/all_to_all | solution.py:136
  527.3 1.3 copy.57
  528.6 6.3 %all-to-all-start.7 = ((bf16[32,8,6,1,384]{4,0,3,2,1:T(8,128)(2,1)}), bf16[32,8,6,1,384]{4,0,3,2,1:T(8,128)(2,1)S(1)}, u32[]{:S(2)}, u32[]{:S(2)}) async-start(bf16[32,8,6,1,384]{4,0,3,2,1:T(8,128)(2,1)} %copy.57), calls=%async_computation.7 | async-start | bytes 2359296 | tf_op jit(solution)/shard_map/all_to_all | solution.py:135
  534.9 1.2 scatter_custom_fusion.2
  536.1 15.3 %all-to-all-done.7 = bf16[32,8,6,1,384]{4,0,3,2,1:T(8,128)(2,1)S(1)} async-done(((bf16[32,8,6,1,384]{4,0,3,2,1:T(8,128)(2,1)}), bf16[32,8,6,1,384]{4,0,3,2,1:T(8,128)(2,1)S(1)}, u32[]{:S(2)}, u32[]{:S(2)}) %all-to-all-start.7) | async-done | bytes 1179680 | tf_op jit(solution)/shard_map/all_to_all | solution.py:135
  552.3 2.3 gather_fusion.9
  (96 shorter events, 10.1 us)
Async XLA Ops:
  0.0 35.8 %copy-start = (bf16[192,3072]{1,0:T(8,128)(2,1)S(1)}, bf16[192,3072]{1,0:T(8,128)(2,1)}, u32[]{:S(2)}) copy-start(bf16[192,3072]{1,0:T(8,128)(2,1)} %param.8) | copy-start | bytes 3538948
  29.4 11.2 %all-to-all-start.3 = ((s32[8,1,576]{2,1,0:T(1,128)}), s32[8,1,576]{2,1,0:T(1,128)}, u32[]{:S(2)}, u32[]{:S(2)}) async-start(s32[8,1,576]{2,1,0:T(1,128)} %reshape.331), calls=%async_computation.3 | async-start | bytes 40960 | tf_op jit(solution)/shard_map/all_to_all | solution.py:70
  37.1 7.6 %copy-start.3 = (bf16[192,3072]{1,0:T(8,128)(2,1)S(1)}, bf16[192,3072]{1,0:T(8,128)(2,1)}, u32[]{:S(2)}) copy-start(bf16[192,3072]{1,0:T(8,128)(2,1)} %param.9) | copy-start | bytes 3538948
  40.6 4.3 copy-start.4
  40.6 33.4 %all-to-all-start.4 = ((bf16[32,6,8,384]{3,2,1,0:T(8,128)(2,1)}), bf16[32,6,8,384]{3,2,1,0:T(8,128)(2,1)S(1)}, u32[]{:S(2)}, u32[]{:S(2)}) async-start(bf16[32,6,8,384]{3,2,1,0:T(8,128)(2,1)} %bitcast.38), calls=%async_computation.4 | async-start | bytes 2359296 | tf_op jit(solution)/shard_map/all_to_all | solution.py:57
  74.0 160.5 %all-to-all-start = ((bf16[32,18,8,768]{3,2,1,0:T(8,128)(2,1)}), bf16[32,18,8,768]{3,2,1,0:T(8,128)(2,1)}, u32[]{:S(2)}, u32[]{:S(2)}) async-start(bf16[32,18,8,768]{3,2,1,0:T(8,128)(2,1)} %fusion.37), calls=%async_computation | async-start | bytes 14155776 | tf_op jit(solution)/shard_map/all_to_all | solution.py:64
  234.5 25.7 %all-to-all-start.5 = ((bf16[32,6,8,384]{3,0,1,2:T(8,128)(2,1)}), bf16[32,6,8,384]{3,0,1,2:T(8,128)(2,1)S(1)}, u32[]{:S(2)}, u32[]{:S(2)}) async-start(bf16[32,6,8,384]{3,0,1,2:T(8,128)(2,1)} %copy.50), calls=%async_computation.5 | async-start | bytes 2359296 | tf_op jit(solution)/shard_map/all_to_all | solution.py:56
  252.0 13.8 %copy-start.2 = (s32[128]{0:T(128)S(1)}, s32[128]{0:T(128)}, u32[]{:S(2)}) copy-start(s32[128]{0:T(128)} %param.13) | copy-start | bytes 1540
  252.0 14.6 %copy-start.5 = (s32[4,4]{1,0:T(4,128)S(1)}, s32[4,4]{1,0:T(4,128)}, u32[]{:S(2)}) copy-start(s32[4,4]{1,0:T(4,128)} %param.12) | copy-start | bytes 196
  260.2 85.4 %all-to-all-start.1 = ((bf16[32,18,8,768]{3,0,1,2:T(8,128)(2,1)}), bf16[32,18,8,768]{3,0,1,2:T(8,128)(2,1)}, u32[]{:S(2)}, u32[]{:S(2)}) async-start(bf16[32,18,8,768]{3,0,1,2:T(8,128)(2,1)} %copy.44), calls=%async_computation.1 | async-start | bytes 14155776 | tf_op jit(solution)/shard_map/all_to_all | solution.py:63
  528.6 22.8 %all-to-all-start.7 = ((bf16[32,8,6,1,384]{4,0,3,2,1:T(8,128)(2,1)}), bf16[32,8,6,1,384]{4,0,3,2,1:T(8,128)(2,1)S(1)}, u32[]{:S(2)}, u32[]{:S(2)}) async-start(bf16[32,8,6,1,384]{4,0,3,2,1:T(8,128)(2,1)} %copy.57), calls=%async_computation.7 | async-start | bytes 2359296 | tf_op jit(solution)/shard_map/all_to_all | solution.py:135
  552.3 2.3 copy-start.1
where the time goes:
time: 557 us; the launch traced here: 555 us
  waiting for transfers between devices  238 us (43%)
  local copies, waits for them, and re-layouts  182 us (33%)
  blocking collectives  61.3 us (11%)
  starting transfers between devices  37.9 us (7%)
  other arithmetic  17.9 us (3%)
  matrix products  16.8 us (3%)
    all_to_all x1, waiting for transfers between devices, body(): lax.all_to_all(wide_pair, 'seq', split_axis=0, concat_axis=0, tiled=True)  153 us
    all_to_all x1, blocking collectives, body(): lax.all_to_all(outgoing, 'seq', split_axis=0, concat_axis=0, tiled=True)  40.7 us
    all_to_all x1, waiting for transfers between devices, body(): lax.all_to_all(lax.all_to_all(wide_pair, 'seq', split_axis=0, concat_axis...  38.6 us
    gather x4, local copies, waits for them, and re-layouts, one_tile(): picked = pair_blocks[windows]  32.2 us
    all_to_all x1, waiting for transfers between devices, body(): lax.all_to_all(query_sorted, 'seq', split_axis=0, concat_axis=0, tiled=True)  21.1 us
    all_to_all x1, blocking collectives, body(): lax.all_to_all(slot_send, 'seq', split_axis=0, concat_axis=0, tiled=True)  20.5 us
    gather x1, local copies, waits for them, and re-layouts, body(): pair_ext = padded[place_ext]  18.8 us
    scatter x1, local copies, waits for them, and re-layouts, body(): place_ext = jnp.full((ext_rows,), 3 * tok_dev, jnp.int32).at[target].set(...  17.6 us
  transfers between devices with their start and end apart: 6, of which 6 were waited for; matrix products, arithmetic and copies ran while one was open for 11% of the time, Pallas kernels for 0%

commit v1 on v0

--- a/solution.py
+++ b/solution.py
@@ -4,6 +4,29 @@
 from jax.sharding import PartitionSpec as P
 
 HEAD_DIM = 128
+
+
+def in_blocks(x, dim, devices):
+    lengths = x.shape
+    blocks = x.reshape(*lengths[:dim], devices, lengths[dim] // devices, *lengths[dim + 1 :])
+    return jnp.moveaxis(blocks, dim, 0)
+
+
+def joined_along(tiles, dim):
+    shape = list(tiles.shape[1:])
+    shape[dim] *= tiles.shape[0]
+    return jnp.moveaxis(tiles, 0, dim).reshape(shape)
+
+
+def exchange_in_pairs(value, axis, split_dim, concat_dim):
+    count, index = (lax.axis_size(axis), lax.axis_index(axis))
+    blocks = in_blocks(value, split_dim, count)
+    gathered = [blocks[index]]
+    for step in range(1, count):
+        sent = blocks[index ^ step]
+        gathered.append(lax.ppermute(sent, axis, [(i, i ^ step) for i in range(count)]))
+    blocks = jnp.stack(gathered)[index ^ jnp.arange(count)]
+    return joined_along(blocks, concat_dim)
 
 
 def body(query, key, value, raster_to_tile, window_list, valid_count):
@@ -67,12 +90,8 @@
             concat_axis=1,
             tiled=True,
         ),
-        lax.all_to_all(
-            lax.all_to_all(slot_send, "seq", split_axis=0, concat_axis=0, tiled=True),
-            "head",
-            split_axis=2,
-            concat_axis=1,
-            tiled=True,
+        exchange_in_pairs(
+            lax.all_to_all(slot_send, "seq", split_axis=0, concat_axis=0, tiled=True), "head", 2, 1
         ),
     )
     middle = slot_in.reshape(seq_count, head_count, 3, share)[:, :, 1, :]

time: 557 us -> 588 us (1.056); the launches traced: 555 us -> 578 us
  waiting for transfers between devices: 238 us -> 252 us
  starting transfers between devices: 37.9 us -> 47.9 us
    ppermute x0 -> x7, waiting for transfers between devices: none -> 66.6 us  [exchange_in_pairs(): lax.ppermute(sent, axis, [(i, i ^ step) for i in range(count)])]
    all_to_all x1, waiting for transfers between devices: 38.6 us -> 0.01 us  [body(): lax.all_to_all(lax.all_to_all(wide_pair, 'seq', split_axis=0, concat_axis...]
    all_to_all x2 -> x1, waiting for transfers between devices: 17.5 us -> 5.93 us  [body(): lax.all_to_all(slot_send, 'seq', split_axis=0, concat_axis=0, tiled=True)]
    ppermute x0 -> x7, starting transfers between devices: none -> 11.4 us  [exchange_in_pairs(): lax.ppermute(sent, axis, [(i, i ^ step) for i in range(count)])]
    all_to_all x2 -> x1, starting transfers between devices: 12.7 us -> 12.2 us  [body(): lax.all_to_all(slot_send, 'seq', split_axis=0, concat_axis=0, tiled=True)]
  transfers between devices with their start and end apart: 6 -> 12, of which waited for: 6 -> 6; matrix products, arithmetic and copies ran while one was open for 11% -> 11% of each run, Pallas kernels for 0% -> 0%
where the time goes in v1:
time: 588 us; the launch traced here: 578 us
  waiting for transfers between devices  252 us (43%)
  local copies, waits for them, and re-layouts  182 us (31%)
  blocking collectives  61.3 us (10%)
  starting transfers between devices  47.9 us (8%)
  other arithmetic  17.2 us (3%)
  matrix products  16.7 us (3%)
    all_to_all x1, waiting for transfers between devices, body(): lax.all_to_all(wide_pair, 'seq', split_axis=0, concat_axis=0, tiled=True)  151 us
    ppermute x7, waiting for transfers between devices, exchange_in_pairs(): lax.ppermute(sent, axis, [(i, i ^ step) for i in range(count)])  66.6 us
    all_to_all x1, blocking collectives, body(): lax.all_to_all(outgoing, 'seq', split_axis=0, concat_axis=0, tiled=True)  38.8 us
    gather x4, local copies, waits for them, and re-layouts, one_tile(): picked = pair_blocks[windows]  32.2 us
    all_to_all x1, blocking collectives, body(): lax.all_to_all(lax.all_to_all(outgoing, 'seq', split_axis=0, concat_axis=...  22.5 us
    all_to_all x1, waiting for transfers between devices, body(): lax.all_to_all(query_sorted, 'seq', split_axis=0, concat_axis=0, tiled=True)  19.5 us
    gather x1, local copies, waits for them, and re-layouts, body(): pair_ext = padded[place_ext]  18.7 us
    scatter x1, local copies, waits for them, and re-layouts, body(): place_ext = jnp.full((ext_rows,), 3 * tok_dev, jnp.int32).at[target].set(...  17.6 us
  transfers between devices with their start and end apart: 12, of which 6 were waited for; matrix products, arithmetic and copies ran while one was open for 11% of the time, Pallas kernels for 0%

profile of v1, /device:TPU:1, one launch (start us, length us, event | category | flops | bytes accessed | tf_op | source)
XLA Modules:
  0.0 577.7 jit_solution(12577039928358637167)
XLA Ops:
  0.0 3.9 sort.17
  4.0 2.0 gather_fusion.4
  7.2 12.2 %all-to-all-start.2 = ((s32[32,1,144]{2,1,0:T(1,128)}), s32[32,1,144]{2,1,0:T(1,128)}, u32[]{:S(2)}, u32[]{:S(2)}) async-start(s32[32,1,144]{2,1,0:T(1,128)} %reshape.380), calls=%async_computation.2 | async-start | bytes 65536 | tf_op jit(solution)/shard_map/all_to_all | solution.py:94
  19.4 1.3 gather_fusion.7
  20.7 1.2 copy.154
  21.9 5.9 %all-to-all-done.2 = s32[32,1,144]{2,1,0:T(1,128)} async-done(((s32[32,1,144]{2,1,0:T(1,128)}), s32[32,1,144]{2,1,0:T(1,128)}, u32[]{:S(2)}, u32[]{:S(2)}) %all-to-all-start.2) | async-done | bytes 18464 | tf_op jit(solution)/shard_map/all_to_all | solution.py:94
  27.9 4.1 all-to-all-start.3
  32.4 1.6 pad_maximum_fusion
  34.0 2.5 gather_fusion.3
  36.8 3.3 fusion.37
  40.2 19.5 %all-to-all-done.3 = bf16[32,6,8,384]{3,2,1,0:T(8,128)(2,1)S(1)} async-done(((bf16[32,6,8,384]{3,2,1,0:T(8,128)(2,1)}), bf16[32,6,8,384]{3,2,1,0:T(8,128)(2,1)S(1)}, u32[]{:S(2)}, u32[]{:S(2)}) %all-to-all-start.3) | async-done | bytes 1179680 | tf_op jit(solution)/shard_map/all_to_all | solution.py:80
  59.7 7.0 %all-to-all-start = ((bf16[32,18,8,768]{3,2,1,0:T(8,128)(2,1)}), bf16[32,18,8,768]{3,2,1,0:T(8,128)(2,1)}, u32[]{:S(2)}, u32[]{:S(2)}) async-start(bf16[32,18,8,768]{3,2,1,0:T(8,128)(2,1)} %fusion.37), calls=%async_computation | async-start | bytes 14155776 | tf_op jit(solution)/shard_map/all_to_all | solution.py:87
  66.6 1.3 copy.125
  67.9 151.4 %all-to-all-done = bf16[32,18,8,768]{3,2,1,0:T(8,128)(2,1)} async-done(((bf16[32,18,8,768]{3,2,1,0:T(8,128)(2,1)}), bf16[32,18,8,768]{3,2,1,0:T(8,128)(2,1)}, u32[]{:S(2)}, u32[]{:S(2)}) %all-to-all-start) | async-done | bytes 7077920 | tf_op jit(solution)/shard_map/all_to_all | solution.py:87
  219.3 7.7 %all-to-all-start.4 = ((bf16[32,6,8,384]{3,0,1,2:T(8,128)(2,1)}), bf16[32,6,8,384]{3,0,1,2:T(8,128)(2,1)S(1)}, u32[]{:S(2)}, u32[]{:S(2)}) async-start(bf16[32,6,8,384]{3,0,1,2:T(8,128)(2,1)} %copy.125), calls=%async_computation.4 | async-start | bytes 2359296 | tf_op jit(solution)/shard_map/all_to_all | solution.py:79
  227.0 8.3 %copy.110 = bf16[32,18,8,768]{3,0,1,2:T(8,128)(2,1)} copy(bf16[32,18,8,768]{3,2,1,0:T(8,128)(2,1)} %all-to-all-done) | data formatting | bytes 14155776 | tf_op jit(solution)/shard_map/all_to_all | solution.py:87
  235.4 8.2 %all-to-all-done.4 = bf16[32,6,8,384]{3,0,1,2:T(8,128)(2,1)S(1)} async-done(((bf16[32,6,8,384]{3,0,1,2:T(8,128)(2,1)}), bf16[32,6,8,384]{3,0,1,2:T(8,128)(2,1)S(1)}, u32[]{:S(2)}, u32[]{:S(2)}) %all-to-all-start.4) | async-done | bytes 1179680 | tf_op jit(solution)/shard_map/all_to_all | solution.py:79
  243.5 5.6 all-to-all-start.1
  249.1 1.2 scatter_custom_fusion.2
  251.7 1.5 reduce.6
  253.8 1.6 collective-permute-start.1
  256.0 2.9 collective-permute-start.3
  259.9 2.7 collective-permute-start.5
  262.6 65.1 %collective-permute-done.1 = s32[32,18,1]{0,1,2:T(8,128)S(1)} collective-permute-done((s32[32,18,1]{0,1,2:T(8,128)S(1)}, s32[32,18,1]{0,1,2:T(8,128)S(1)}, u32[]{:S(2)}, u32[]{:S(2)}) %collective-permute-start.1) | collective-permute-done | bytes 2336 | tf_op jit(solution)/shard_map/ppermute | solution.py:27
  327.7 2.8 collective-permute-start.6
  330.6 1.5 collective-permute-done.6
  333.7 6.2 %scatter_custom_fusion.1 = s32[1536]{0:T(1024)S(1)} fusion(s32[1536]{0:T(1024)S(1)} %fusion.42, s32[1536]{0:T(1024)S(1)} %iota.29, s32[]{:T(128)} %copy.186), kind=kCustom, calls=%fused_computation.80 | custom fusion | bytes 6148 | tf_op jit(solution)/shard_map/scatter | solution.py:99
  340.0 17.6 %scatter_custom_fusion = s32[3840]{0:T(1024)S(1)} fusion(s32[4608]{0:T(1024)S(1)} %fusion.39, s32[4608]{0:T(1024)S(1)} %iota.28, s32[]{:T(128)} %constant.21.clone.1), kind=kCustom, calls=%fused_computation.72 | custom fusion | bytes 15364 | tf_op jit(solution)/shard_map/scatter | solution.py:107
  357.7 1.7 copy.126
  359.3 2.3 reshape.239
  361.6 5.3 gather_fusion.8
  367.0 3.3 reshape.370
  370.2 1.3 copy.129
  371.5 10.9 %copy.111 = bf16[32,8,18,1,768]{4,2,1,0,3:T(8,128)(2,1)} copy(bf16[32,8,18,1,768]{4,0,2,1,3:T(8,128)(2,1)} %bitcast.5) | data formatting | bytes 14155776 | tf_op jit(solution)/shard_map/all_to_all | solution.py:86
  382.4 11.5 %reshape.235 = bf16[4608,768]{1,0:T(8,128)(2,1)} reshape(bf16[32,8,18,1,768]{4,2,1,0,3:T(8,128)(2,1)} %copy.111) | data formatting | bytes 14155776 | tf_op jit(solution)/shard_map/reshape | solution.py:111
  393.9 6.4 %concatenate.28 = bf16[4609,768]{1,0:T(8,128)(2,1)} pad(bf16[4608,768]{1,0:T(8,128)(2,1)} %reshape.235, bf16[]{:T(256)} %constant.38.clone.1), padding=0_1x0_0 | pad | bytes 14157314 | tf_op jit(solution)/shard_map/concatenate | solution.py:109
  400.3 18.7 %gather_fusion.6 = bf16[3840,768]{1,0:T(8,128)(2,1)} fusion(bf16[4609,768]{1,0:T(8,128)(2,1)} %concatenate.28, s32[4096]{0:T(1024)S(1)} %pad_clamp_fusion.1), kind=kCustom, calls=%fused_computation.6 | custom fusion | bytes 11811840 | tf_op jit(solution)/shard_map/gather | solution.py:116
  419.0 13.8 %reshape.237 = bf16[10,384,2,3,128]{4,3,2,1,0:T(4,128)(2,1)} reshape(bf16[3840,768]{1,0:T(8,128)(2,1)} %gather_fusion.6) | data formatting | bytes 11796480 | tf_op jit(solution)/shard_map/reshape | solution.py:123
  432.8 72.1 %while.11 = (s32[]{:T(128)}, bf16[4,384,384]{2,1,0:T(8,128)(2,1)S(1)}, pred[4,384]{1,0:T(4,128)(4,1)S(1)}, s32[4,4]{1,0:T(4,128)S(1)}, bf16[10,384,2,3,128]{4,3,...) while((s32[]{:T(128)}, ...), condition=%wide.region_6.7_spmd.clone, body=%wide.region_3.6_spmd.clone.sunk | while | flops 925878784 | bytes 37202520 | solution.py:150
  433.7 8.1 %gather_fusion.1 = bf16[4,384,2,3,128]{4,3,2,1,0:T(4,128)(2,1)} fusion(bf16[10,384,2,3,128]{4,3,2,1,0:T(4,128)(2,1)} %get-tuple-element.211, s32[1024]{0:T(1024)S(1)} %pad_clamp_fusion.9), kind=kCustom, calls=%fused_computation.clone.clone.1 | custom fusion | bytes 4718608 | tf_op jit(solution)/shard_map/while/body/eval_jaxpr/gather | solution.py:128
  441.8 3.0 fusion.65
  445.0 2.2 fusion.66
  447.1 1.5 fusion.67
  448.7 2.0 fusion.68
  451.7 8.1 %gather_fusion.1 = bf16[4,384,2,3,128]{4,3,2,1,0:T(4,128)(2,1)} fusion(bf16[10,384,2,3,128]{4,3,2,1,0:T(4,128)(2,1)} %get-tuple-element.211, s32[1024]{0:T(1024)S(1)} %pad_clamp_fusion.9), kind=kCustom, calls=%fused_computation.clone.clone.1 | custom fusion | bytes 4718608 | tf_op jit(solution)/shard_map/while/body/eval_jaxpr/gather | solution.py:128
  459.8 3.0 fusion.65
  463.0 2.2 fusion.66
  465.1 1.5 fusion.67
  466.7 2.0 fusion.68
  469.7 8.1 %gather_fusion.1 = bf16[4,384,2,3,128]{4,3,2,1,0:T(4,128)(2,1)} fusion(bf16[10,384,2,3,128]{4,3,2,1,0:T(4,128)(2,1)} %get-tuple-element.211, s32[1024]{0:T(1024)S(1)} %pad_clamp_fusion.9), kind=kCustom, calls=%fused_computation.clone.clone.1 | custom fusion | bytes 4718608 | tf_op jit(solution)/shard_map/while/body/eval_jaxpr/gather | solution.py:128
  477.7 3.0 fusion.65
  480.9 2.2 fusion.66
  483.1 1.5 fusion.67
  484.6 2.0 fusion.68
  487.7 8.1 %gather_fusion.1 = bf16[4,384,2,3,128]{4,3,2,1,0:T(4,128)(2,1)} fusion(bf16[10,384,2,3,128]{4,3,2,1,0:T(4,128)(2,1)} %get-tuple-element.211, s32[1024]{0:T(1024)S(1)} %pad_clamp_fusion.9), kind=kCustom, calls=%fused_computation.clone.clone.1 | custom fusion | bytes 4718608 | tf_op jit(solution)/shard_map/while/body/eval_jaxpr/gather | solution.py:128
  495.7 3.0 fusion.65
  498.9 2.2 fusion.66
  501.1 1.5 fusion.67
  502.6 2.0 fusion.68
  504.9 5.3 gather_fusion.9
  510.2 2.2 reshape.242
  512.7 38.8 %all_to_all.65 = bf16[32,8,6,1,384]{4,1,3,2,0:T(8,128)(2,1)S(1)} all-to-all(bf16[32,8,6,1,384]{4,1,3,2,0:T(8,128)(2,1)S(1)} %copy.131), channel_id=1, replica_groups=mesh['seq'=32,'head'=8] {'seq'}, dimensions={0} | all-to-all | bytes 2359296 | tf_op jit(solution)/shard_map/all_to_all | solution.py:155
  551.7 22.5 %all_to_all.66 = bf16[32,8,6,1,384]{4,0,3,2,1:T(8,128)(2,1)S(1)} all-to-all(bf16[32,8,6,1,384]{4,0,3,2,1:T(8,128)(2,1)S(1)} %copy.132), channel_id=1, replica_groups=mesh['seq'=32,'head'=8] {'head'}, dimensions={1} | all-to-all | bytes 2359296 | tf_op jit(solution)/shard_map/all_to_all | solution.py:154
  575.1 2.3 gather_fusion.10
  (122 shorter events, 13.4 us)
Async XLA Ops:
  0.0 19.4 %copy-start = (bf16[192,3072]{1,0:T(8,128)(2,1)S(1)}, bf16[192,3072]{1,0:T(8,128)(2,1)}, u32[]{:S(2)}) copy-start(bf16[192,3072]{1,0:T(8,128)(2,1)} %param.8) | copy-start | bytes 3538948
  7.2 20.7 %all-to-all-start.2 = ((s32[32,1,144]{2,1,0:T(1,128)}), s32[32,1,144]{2,1,0:T(1,128)}, u32[]{:S(2)}, u32[]{:S(2)}) async-start(s32[32,1,144]{2,1,0:T(1,128)} %reshape.380), calls=%async_computation.2 | async-start | bytes 65536 | tf_op jit(solution)/shard_map/all_to_all | solution.py:94
  20.7 11.3 %copy-start.3 = (bf16[192,3072]{1,0:T(8,128)(2,1)S(1)}, bf16[192,3072]{1,0:T(8,128)(2,1)}, u32[]{:S(2)}) copy-start(bf16[192,3072]{1,0:T(8,128)(2,1)} %param.9) | copy-start | bytes 3538948
  27.9 4.3 copy-start.4
  27.9 31.8 %all-to-all-start.3 = ((bf16[32,6,8,384]{3,2,1,0:T(8,128)(2,1)}), bf16[32,6,8,384]{3,2,1,0:T(8,128)(2,1)S(1)}, u32[]{:S(2)}, u32[]{:S(2)}) async-start(bf16[32,6,8,384]{3,2,1,0:T(8,128)(2,1)} %bitcast.48), calls=%async_computation.3 | async-start | bytes 2359296 | tf_op jit(solution)/shard_map/all_to_all | solution.py:80
  59.7 159.6 %all-to-all-start = ((bf16[32,18,8,768]{3,2,1,0:T(8,128)(2,1)}), bf16[32,18,8,768]{3,2,1,0:T(8,128)(2,1)}, u32[]{:S(2)}, u32[]{:S(2)}) async-start(bf16[32,18,8,768]{3,2,1,0:T(8,128)(2,1)} %fusion.37), calls=%async_computation | async-start | bytes 14155776 | tf_op jit(solution)/shard_map/all_to_all | solution.py:87
  219.3 24.2 %all-to-all-start.4 = ((bf16[32,6,8,384]{3,0,1,2:T(8,128)(2,1)}), bf16[32,6,8,384]{3,0,1,2:T(8,128)(2,1)S(1)}, u32[]{:S(2)}, u32[]{:S(2)}) async-start(bf16[32,6,8,384]{3,0,1,2:T(8,128)(2,1)} %copy.125), calls=%async_computation.4 | async-start | bytes 2359296 | tf_op jit(solution)/shard_map/all_to_all | solution.py:79
  235.4 15.0 %copy-start.2 = (s32[128]{0:T(128)S(1)}, s32[128]{0:T(128)}, u32[]{:S(2)}) copy-start(s32[128]{0:T(128)} %param.13) | copy-start | bytes 1540
  235.4 15.8 %copy-start.5 = (s32[4,4]{1,0:T(4,128)S(1)}, s32[4,4]{1,0:T(4,128)}, u32[]{:S(2)}) copy-start(s32[4,4]{1,0:T(4,128)} %param.12) | copy-start | bytes 196
  243.5 128.0 %all-to-all-start.1 = ((bf16[32,18,8,768]{3,0,1,2:T(8,128)(2,1)}), bf16[32,18,8,768]{3,0,1,2:T(8,128)(2,1)}, u32[]{:S(2)}, u32[]{:S(2)}) async-start(bf16[32,18,8,768]{3,0,1,2:T(8,128)(2,1)} %copy.110), calls=%async_computation.1 | async-start | bytes 14155776 | tf_op jit(solution)/shard_map/all_to_all | solution.py:86
  253.6 6.3 %collective-permute-start = (s32[32,18,1]{0,1,2:T(8,128)S(1)}, s32[32,18,1]{0,1,2:T(8,128)S(1)}, u32[]{:S(2)}, u32[]{:S(2)}) collective-permute-start(s32[32,18,1]{0,1,2:T(8,128)S(1)} %copy.143), channel_id=1, source_target_pairs={{0,1},{1,0},{2,3},{3,2},{4,5},{5,4},{6,7},{7,6},{8,9},{9,8},{10,11... | collective-permute-start | bytes 6920 | tf_op jit(solution)/shard_map/ppermute | solution.py:27
  253.8 73.8 %collective-permute-start.1 = (s32[32,18,1]{0,1,2:T(8,128)S(1)}, s32[32,18,1]{0,1,2:T(8,128)S(1)}, u32[]{:S(2)}, u32[]{:S(2)}) collective-permute-start(s32[32,18,1]{0,1,2:T(8,128)S(1)} %copy.144), channel_id=1, source_target_pairs={{0,2},{1,3},{2,0},{3,1},{4,6},{5,7},{6,4},{7,5},{8,10},{9,11},{10,... | collective-permute-start | bytes 6920 | tf_op jit(solution)/shard_map/ppermute | solution.py:27
  255.5 75.0 %collective-permute-start.2 = (s32[32,18,1]{0,1,2:T(8,128)S(1)}, s32[32,18,1]{0,1,2:T(8,128)S(1)}, u32[]{:S(2)}, u32[]{:S(2)}) collective-permute-start(s32[32,18,1]{0,1,2:T(8,128)S(1)} %copy.145), channel_id=1, source_target_pairs={{0,3},{1,2},{2,1},{3,0},{4,7},{5,6},{6,5},{7,4},{8,11},{9,10},{10,... | collective-permute-start | bytes 6920 | tf_op jit(solution)/shard_map/ppermute | solution.py:27
  256.0 74.5 %collective-permute-start.3 = (s32[32,18,1]{0,1,2:T(8,128)S(1)}, s32[32,18,1]{0,1,2:T(8,128)S(1)}, u32[]{:S(2)}, u32[]{:S(2)}) collective-permute-start(s32[32,18,1]{0,1,2:T(8,128)S(1)} %copy.146), channel_id=1, source_target_pairs={{0,4},{1,5},{2,6},{3,7},{4,0},{5,1},{6,2},{7,3},{8,12},{9,13},{10,... | collective-permute-start | bytes 6920 | tf_op jit(solution)/shard_map/ppermute | solution.py:27
  259.0 71.5 %collective-permute-start.4 = (s32[32,18,1]{0,1,2:T(8,128)S(1)}, s32[32,18,1]{0,1,2:T(8,128)S(1)}, u32[]{:S(2)}, u32[]{:S(2)}) collective-permute-start(s32[32,18,1]{0,1,2:T(8,128)S(1)} %copy.147), channel_id=1, source_target_pairs={{0,5},{1,4},{2,7},{3,6},{4,1},{5,0},{6,3},{7,2},{8,13},{9,12},{10,... | collective-permute-start | bytes 6920 | tf_op jit(solution)/shard_map/ppermute | solution.py:27
  259.9 72.2 %collective-permute-start.5 = (s32[32,18,1]{0,1,2:T(8,128)S(1)}, s32[32,18,1]{0,1,2:T(8,128)S(1)}, u32[]{:S(2)}, u32[]{:S(2)}) collective-permute-start(s32[32,18,1]{0,1,2:T(8,128)S(1)} %copy.148), channel_id=1, source_target_pairs={{0,6},{1,7},{2,4},{3,5},{4,2},{5,3},{6,0},{7,1},{8,14},{9,15},{10,... | collective-permute-start | bytes 6920 | tf_op jit(solution)/shard_map/ppermute | solution.py:27
  327.7 4.4 collective-permute-start.6
  575.1 2.3 copy-start.1
